TPU v7x, 32 devices: a whole 2x2x4 slice. The times are simulated.
32 devices in a mesh: seq: 16 (over z, y, core), head: 2 (over x).
Axes of the slice: x: 2, y: 2, z: 4, core: 2. Of those that a mesh axis runs over, the one named last changes fastest.
Arguments:
- queries: bfloat16 [8192, 4096], P(('seq', 'head')), may hold values from -6 to 6
- keys: bfloat16 [8192, 4096], P(('seq', 'head')), may hold values from -6 to 6
- values: bfloat16 [8192, 4096], P(('seq', 'head')), may hold values from -6 to 6
- cluster_ids: int32 [32, 8192, 1], P(None, 'seq'), may hold values from 0 to 127; in each aligned block of 256 rows (0 to 255, 256 to 511, ..., all dimensions but the last counted through in order) at most 4 rows name the same one
- out_weight: bfloat16 [4096, 4096], P('head', 'seq'), may hold values from -0.09375 to 0.09375
Outputs:
- projected: bfloat16 [8192, 4096], P('seq', 'head')
Inputs may be any that keep to these rules, and one draw needn't show every extreme that they name: `cluster_ids`: in each aligned block of 256 tokens of one head (the rows of one device), no cluster id appears more than 4 times, and some cluster appears exactly 4 times.
All inputs are finite; a program needn't handle non-finite values.
Results may differ from a plain program's by a relative error of at most 0.014.
Values may be sent and summed in bfloat16 or wider, within the bound.
A program may use at most 128 MiB of HBM per device.

v0:
```python
import jax
import jax.numpy as jnp
from jax import lax
from jax.sharding import PartitionSpec as P

HEADS = 32
HD = 128
CLUSTERS = 128


def slot_table(block_ids, slot_depth):
    sub_rows = block_ids.shape[-1]
    onehot = (block_ids[..., None] == jnp.arange(CLUSTERS, dtype=jnp.int32)).astype(jnp.float32)
    lower = (jnp.arange(sub_rows)[:, None] >= jnp.arange(sub_rows)[None, :]).astype(jnp.float32)
    running = jnp.einsum("ts,abse->abte", lower, onehot)
    ranking = (jnp.sum(running * onehot, axis=-1) - 1.0).astype(jnp.int32)
    depth_hit = (ranking[..., None] == jnp.arange(slot_depth, dtype=jnp.int32)).astype(jnp.bfloat16)
    return onehot.astype(jnp.bfloat16)[..., :, None] * depth_hit[..., None, :]


def attend_blocks(packed, validity):
    scores = jnp.einsum(
        "cqd,ckd->cqk", packed[0], packed[1], preferred_element_type=jnp.float32
    ) * HD ** (-0.5)
    scores = jnp.where(validity[:, None, :] > 0, scores, -1e30)
    row_max = jnp.max(scores, axis=-1, keepdims=True)
    raised = jnp.exp(scores - row_max)
    weights = (raised / jnp.sum(raised, axis=-1, keepdims=True)).astype(jnp.bfloat16)
    return jnp.einsum(
        "cqk,ckd->cqd", weights, packed[2], preferred_element_type=jnp.float32
    ).astype(jnp.bfloat16)


def attend_and_return(arrived):
    packed, markers = arrived
    item_count = packed.shape[1]
    n_seq = packed.shape[2]
    lane_count = packed.shape[3]
    result_block = attend_blocks(
        packed.reshape(3, item_count, n_seq * lane_count, HD),
        markers.reshape(item_count, n_seq * lane_count),
    )
    result_block = result_block.reshape(item_count, n_seq, lane_count, HD)
    return lax.all_to_all(result_block, "seq", split_axis=1, concat_axis=1, tiled=True)


def body(queries, keys, values, cluster_ids, out_weight):
    n_seq = lax.axis_size("seq")
    n_head = lax.axis_size("head")
    head_group = lax.axis_index("head")
    tok_dev = cluster_ids.shape[1]
    sub_rows = tok_dev // n_head
    group_heads = HEADS // n_head
    slot_depth = max(2, 2 * tok_dev // (n_head * CLUSTERS))
    lane_count = n_head * slot_depth
    per_owner = group_heads * CLUSTERS // n_seq
    all_ids = cluster_ids[:, :, 0]
    group_ids = lax.dynamic_slice_in_dim(all_ids, head_group * group_heads, group_heads, 0)
    group_ids = group_ids.reshape(group_heads, n_head, sub_rows)
    home_table = slot_table(group_ids, slot_depth)
    relaid = (
        lax.all_to_all(queries, "head", split_axis=1, concat_axis=0, tiled=True),
        lax.all_to_all(keys, "head", split_axis=1, concat_axis=0, tiled=True),
        lax.all_to_all(values, "head", split_axis=1, concat_axis=0, tiled=True),
    )
    stacked = jnp.stack([tensor.reshape(n_head, sub_rows, group_heads, HD) for tensor in relaid])
    packed = jnp.einsum(
        "hltcr,xlthd->xhclrd", home_table, stacked, preferred_element_type=jnp.float32
    ).astype(jnp.bfloat16)
    packed = packed.reshape(3, per_owner, n_seq, lane_count, HD)
    markers = (
        jnp.sum(home_table.astype(jnp.float32), axis=2).transpose(0, 2, 1, 3).astype(jnp.bfloat16)
    )
    markers = markers.reshape(1, per_owner, n_seq, lane_count)
    returned = attend_and_return(
        (
            lax.all_to_all(packed, "seq", split_axis=2, concat_axis=2, tiled=True),
            lax.all_to_all(markers, "seq", split_axis=2, concat_axis=2, tiled=True),
        )
    )
    returned = returned.reshape(group_heads, CLUSTERS, n_head, slot_depth, HD)
    gathered = jnp.einsum(
        "hltcr,hclrd->lthd", home_table, returned, preferred_element_type=jnp.float32
    ).astype(jnp.bfloat16)
    gathered = gathered.reshape(tok_dev, group_heads * HD)
    partial_value = jnp.dot(
        gathered,
        lax.all_gather(out_weight, "seq", axis=1, tiled=True),
        preferred_element_type=jnp.float32,
    )
    return lax.psum_scatter(
        partial_value.astype(jnp.bfloat16), "head", scatter_dimension=1, tiled=True
    )


def solution(mesh):
    in_specs = (
        P(("seq", "head"), None),
        P(("seq", "head"), None),
        P(("seq", "head"), None),
        P(None, "seq", None),
        P("head", "seq"),
    )
    out_specs = P("seq", "head")
    return jax.shard_map(body, mesh=mesh, in_specs=in_specs, out_specs=out_specs, check_vma=False)
```

profile of v0, /device:TPU:0, one launch (start us, length us, event | category | flops | bytes accessed | tf_op | source)
XLA Modules:
  0.0 741.0 jit_solution(9543671924512516309)
XLA Ops:
  6.5 0.0 copy-start
  6.5 4.1 copy.56
  10.6 4.2 all-to-all-start.1
  14.8 4.1 copy.57
  18.9 21.8 %all-to-all-done.1 = bf16[256,2,2048]{0,2,1:T(8,128)(2,1)S(1)} async-done(((bf16[256,2,2048]{0,2,1:T(8,128)(2,1)}), bf16[256,2,2048]{0,2,1:T(8,128)(2,1)S(1)}, u32[]{:S(2)}, u32[]{:S(2)}) %all-to-all-start.1) | async-done | bytes 2097184 | tf_op jit(solution)/shard_map/all_to_all | solution.py:62
  40.7 0.0 copy-start.2
  40.7 4.8 all-to-all-start.2
  45.5 0.0 copy-done
  45.5 0.1 dynamic-slice_reduce_fusion
  45.6 4.1 copy.58
  49.7 0.0 copy-done.2
  49.7 2.1 convert_convert_fusion
  51.8 18.3 %all-to-all-done.2 = bf16[256,2,2048]{0,2,1:T(8,128)(2,1)} async-done(((bf16[256,2,2048]{0,2,1:T(8,128)(2,1)}), bf16[256,2,2048]{0,2,1:T(8,128)(2,1)}, u32[]{:S(2)}, u32[]{:S(2)}) %all-to-all-start.2) | async-done | bytes 2097184 | tf_op jit(solution)/shard_map/all_to_all | solution.py:63
  70.1 4.8 all-to-all-start.3
  75.0 1.3 fusion.18
  76.3 3.0 copy.50
  79.4 6.1 multiply_reduce_fusion
  85.5 0.2 reshape.61
  85.7 0.7 copy.53
  86.5 3.9 copy.59
  90.4 4.0 copy.60
  94.4 4.3 all-to-all-done.3
  98.7 5.6 all-to-all-start
  104.2 3.9 copy.61
  108.2 10.6 %convert_bitcast_fusion = bf16[3,16,128,2,4,128]{5,2,4,0,3,1:T(8,128)(2,1)} fusion(bf16[16,2,256,128,4,1]{3,2,4,0,1,5:T(8,128)(2,1)} %get-tuple-element.9, bf16[1,2,256,16,128]{4,2,0,1,3:T(8,128)(2,1)} %copy.61, bf16[1,2,256,16,128]{4,2,0,1,3:T(8,128)(2,1)} %copy.60, bf16[1,2,256,16,128]{4,2,0,1,3:T(8,128)(2,1)} %copy.59), kind=kOutput, calls=%fused_computation.5 | convolution fusion | flops 3246391296 | bytes 27262976 | tf_op jit(solution)/shard_map/hltcr,xlthd->xhclrd/dot_general | solution.py:67
  118.8 6.2 copy.63
  125.0 8.4 %copy.64 = bf16[3,128,16,8,128]{4,1,3,0,2:T(8,128)(2,1)} copy(bf16[3,128,16,8,128]{4,2,1,3,0:T(8,128)(2,1)S(1)} %bitcast.67) | data formatting | bytes 25165824 | tf_op jit(solution)/shard_map/reshape | solution.py:70
  133.4 0.0 all-to-all-done
  133.4 6.1 all-to-all-start.4
  139.4 0.0 all-gather.2.cloned.1.call-start
  139.5 0.7 all-gather.2.cloned.1.call-update
  140.2 0.2 reduce-scatter.2.cloned.1.call-start
  140.4 0.1 copy.55
  140.5 323.8 %all-to-all-done.4 = bf16[3,128,16,8,128]{4,1,3,0,2:T(8,128)(2,1)} async-done(((bf16[3,128,16,8,128]{4,1,3,0,2:T(8,128)(2,1)}), bf16[3,128,16,8,128]{4,1,3,0,2:T(8,128)(2,1)}, u32[]{:S(2)}, u32[]{:S(2)}) %all-to-all-start.4) | async-done | bytes 12582944 | tf_op jit(solution)/shard_map/all_to_all | solution.py:77
  464.3 7.8 %fusion.46 = (bf16[1,128,16,8,128]{4,1,3,0,2:T(8,128)(2,1)S(1)}, bf16[1,128,16,8,128]{4,1,3,0,2:T(8,128)(2,1)}, bf16[1,128,16,8,128]{4,1,3,0,2:T(8,128)(2,1)S(1)}) fusion(bf16[3,128,16,8,128]{4,1,3,0,2:T(8,128)(2,1)} %all-to-all-done.4), kind=kLoop, calls=%fused_computation.55 | loop fusion | bytes 25165824 | tf_op jit(solution)/shard_map/slice | solution.py:23
  472.1 8.6 %fusion.15 = f32[128,128,128]{1,2,0:T(8,128)} fusion(bf16[1,128,16,8,128]{4,1,3,0,2:T(8,128)(2,1)S(1)} %get-tuple-element.7, bf16[1,128,16,8,128]{4,1,3,0,2:T(8,128)(2,1)S(1)} %get-tuple-element.5), kind=kOutput, calls=%fused_computation.22 | convolution fusion | flops 536870912 | bytes 16777216 | tf_op jit(solution)/shard_map/cqd,ckd->cqk/dot_general | solution.py:22
  480.8 13.4 %fusion.47 = (f32[128,128]{1,0:T(8,128)S(1)}, f32[128,128,128]{1,2,0:T(8,128)}) fusion(f32[128,128,128]{1,2,0:T(8,128)} %fusion.15, pred[128,128]{1,0:T(8,128)(4,1)S(1)} %copy.55), kind=kOutput, calls=%fused_computation.56 | output fusion | flops 12583039 | bytes 16859136 | tf_op jit(solution)/shard_map/sub | solution.py:27
  494.1 9.2 %convert_bitcast_fusion.1 = bf16[128,16,8,128]{3,2,1,0:T(8,128)(2,1)S(1)} fusion(bf16[1,128,16,8,128]{4,1,3,0,2:T(8,128)(2,1)} %get-tuple-element.6, f32[128,128,128]{1,2,0:T(8,128)} %get-tuple-element.11, f32[128,128]{1,0:T(8,128)S(1)} %get-tuple-element.10), kind=kOutput, calls=%fused_computation.30 | convolution fusion | flops 543162368 | bytes 16842752 | tf_op jit(solution)/shard_map/cqk,ckd->cqd/dot_general | solution.py:29
  503.3 2.7 copy.69
  506.0 145.4 %all_to_all.63 = bf16[128,16,8,128]{3,0,2,1:T(8,128)(2,1)S(1)} all-to-all(bf16[128,16,8,128]{3,0,2,1:T(8,128)(2,1)S(1)} %copy.69), channel_id=1, replica_groups=mesh['seq'=16,'head'=2] {'seq'}, dimensions={1} | all-to-all | bytes 8388608 | tf_op jit(solution)/shard_map/all_to_all | solution.py:44
  651.4 2.7 copy.70
  654.1 8.5 %fusion.31 = bf16[2,256,16,128]{1,3,2,0:T(8,128)(2,1)} fusion(bf16[16,2,256,4]{2,3,0,1:T(4,128)(2,1)S(1)} %fusion.41, bf16[16,2,256,128]{3,2,0,1:T(8,128)(2,1)S(1)} %copy.50, bf16[16,128,2,4,128]{4,1,0,3,2:T(8,128)(2,1)S(1)} %bitcast.72), kind=kOutput, calls=%fused_computation.40 | convolution fusion | flops 1078984704 | bytes 8454144 | tf_op jit(solution)/shard_map/hltcr,hclrd->lthd/dot_general | solution.py:82
  662.6 3.4 copy.72
  666.1 0.0 all-gather.2.cloned.1.call-done
  666.1 0.0 copy-start.1
  666.1 13.8 %convolution_convert_fusion = bf16[512,4096]{1,0:T(8,128)(2,1)} fusion(bf16[2048,4096]{1,0:T(8,128)(2,1)} %all-gather.2.cloned.1.call-done, bf16[64,8,16,128]{3,2,1,0:T(8,128)(2,1)S(1)} %bitcast.73), kind=kOutput, calls=%fused_computation.17 | convolution fusion | flops 8592031744 | bytes 23068672 | tf_op jit(solution)/shard_map/dot_general | solution.py:86
  680.0 0.0 reduce-scatter.2.cloned.1.call-update
  680.0 54.1 %reduce-scatter.2.cloned.1.call-done = bf16[512,2048]{1,0:T(8,128)(2,1)} async-done(((bf16[512,4096]{1,0:T(8,128)(2,1)}), bf16[512,2048]{1,0:T(8,128)(2,1)}) %reduce-scatter.2.cloned.1.call-update) | async-done | bytes 2097168 | tf_op jit(solution)/shard_map/reduce_scatter | solution.py:91
  734.1 0.0 copy-done.1
  (5 shorter events, 0.1 us)
Async XLA Ops:
  6.5 39.0 %copy-start = (s32[32,512,1]{1,2,0:T(1,128)S(1)}, s32[32,512,1]{1,2,0:T(1,128)}, u32[]{:S(2)}) copy-start(s32[32,512,1]{1,2,0:T(1,128)} %param.8) | copy-start | bytes 196612
  10.6 30.1 %all-to-all-start.1 = ((bf16[256,2,2048]{0,2,1:T(8,128)(2,1)}), bf16[256,2,2048]{0,2,1:T(8,128)(2,1)S(1)}, u32[]{:S(2)}, u32[]{:S(2)}) async-start(bf16[256,2,2048]{0,2,1:T(8,128)(2,1)} %bitcast.71), calls=%async_computation.1 | async-start | bytes 4194304 | tf_op jit(solution)/shard_map/all_to_all | solution.py:62
  40.7 9.0 %copy-start.2 = (bf16[256,2,2048]{0,2,1:T(8,128)(2,1)}, bf16[256,2,2048]{0,2,1:T(8,128)(2,1)S(1)}, u32[]{:S(2)}) copy-start(bf16[256,2,2048]{0,2,1:T(8,128)(2,1)S(1)} %all-to-all-done.1) | copy-start | bytes 6291460
  40.7 29.4 %all-to-all-start.2 = ((bf16[256,2,2048]{0,2,1:T(8,128)(2,1)}), bf16[256,2,2048]{0,2,1:T(8,128)(2,1)}, u32[]{:S(2)}, u32[]{:S(2)}) async-start(bf16[256,2,2048]{0,2,1:T(8,128)(2,1)} %bitcast.69), calls=%async_computation.2 | async-start | bytes 4194304 | tf_op jit(solution)/shard_map/all_to_all | solution.py:63
  70.1 28.5 %all-to-all-start.3 = ((bf16[256,2,2048]{0,2,1:T(8,128)(2,1)}), bf16[256,2,2048]{0,2,1:T(8,128)(2,1)}, u32[]{:S(2)}, u32[]{:S(2)}) async-start(bf16[256,2,2048]{0,2,1:T(8,128)(2,1)} %bitcast.70), calls=%async_computation.3 | async-start | bytes 4194304 | tf_op jit(solution)/shard_map/all_to_all | solution.py:64
  98.7 34.7 %all-to-all-start = ((bf16[1,128,16,8]{1,3,0,2:T(8,128)(2,1)}), bf16[1,128,16,8]{1,3,0,2:T(8,128)(2,1)S(1)}, u32[]{:S(2)}, u32[]{:S(2)}) async-start(bf16[1,128,16,8]{1,3,0,2:T(8,128)(2,1)} %copy.53), calls=%async_computation | async-start | bytes 65536 | tf_op jit(solution)/shard_map/all_to_all | solution.py:78
  133.4 331.0 %all-to-all-start.4 = ((bf16[3,128,16,8,128]{4,1,3,0,2:T(8,128)(2,1)}), bf16[3,128,16,8,128]{4,1,3,0,2:T(8,128)(2,1)}, u32[]{:S(2)}, u32[]{:S(2)}) async-start(bf16[3,128,16,8,128]{4,1,3,0,2:T(8,128)(2,1)} %copy.64), calls=%async_computation.4 | async-start | bytes 25165824 | tf_op jit(solution)/shard_map/all_to_all | solution.py:77
  139.4 526.7 %all-gather.2.cloned.1.call-start = ((), (), s32[]{:S(2)}) async-start(), calls=%async_computation.7 | async-start | bytes 17825792 | tf_op jit(solution)/shard_map/all_gather | solution.py:88
  140.2 594.0 %reduce-scatter.2.cloned.1.call-start = ((), (), s32[]{:S(2)}) async-start(), calls=%async_computation.8 | async-start | bytes 6291456 | tf_op jit(solution)/shard_map/reduce_scatter | solution.py:91
  666.1 68.0 %copy-start.1 = (s32[32,512,1]{1,2,0:T(1,128)S(1)}, s32[32,512,1]{1,2,0:T(1,128)}, u32[]{:S(2)}) copy-start(s32[32,512,1]{1,2,0:T(1,128)} %param.8) | copy-start | bytes 196612
Sparse Core Ops, SparseCore 0:
  142.4 322.0 all-gather.1
  680.1 53.9 reduce-scatter.1
where the time goes:
time: 742 us; the launch traced here: 741 us
  waiting for transfers between devices  423 us (57%)
  blocking collectives  145 us (20%)
  local copies, waits for them, and re-layouts  59.5 us (8%)
  matrix products  52.1 us (7%)
  starting transfers between devices  25.7 us (3%)
  other arithmetic  21.6 us (3%)
  between operations  13.6 us (2%)
    all_to_all x1, waiting for transfers between devices, body(): lax.all_to_all(packed, 'seq', split_axis=2, concat_axis=2, tiled=True)  324 us
    all_to_all x1, blocking collectives, attend_and_return(): lax.all_to_all(result_block, 'seq', split_axis=1, concat_axis=1, tiled=True)  145 us
    reduce_scatter x1, waiting for transfers between devices, body(): lax.psum_scatter(partial_value.astype(jnp.bfloat16), 'head', scatter_dime...  54.1 us
    all_to_all x1, waiting for transfers between devices, body(): lax.all_to_all(queries, 'head', split_axis=1, concat_axis=0, tiled=True)  21.8 us
    all_to_all x1, waiting for transfers between devices, body(): lax.all_to_all(keys, 'head', split_axis=1, concat_axis=0, tiled=True)  18.3 us
  transfers between devices with their start and end apart: 7, of which 5 were waited for; matrix products, arithmetic and copies ran while one was open for 16% of the time, Pallas kernels for 0%

commit v1 on v0

--- a/solution.py
+++ b/solution.py
@@ -44,7 +44,7 @@
     return lax.all_to_all(result_block, "seq", split_axis=1, concat_axis=1, tiled=True)
 
 
-def body(queries, keys, values, cluster_ids, out_weight):
+def generic_body(queries, keys, values, cluster_ids, out_weight):
     n_seq = lax.axis_size("seq")
     n_head = lax.axis_size("head")
     head_group = lax.axis_index("head")
@@ -93,6 +93,58 @@
     )
 
 
+def head_slots(block_ids, most):
+    onehot = block_ids[:, None, :] == jnp.arange(CLUSTERS, dtype=jnp.int32)[None, :, None]
+    rows = block_ids.shape[-1]
+    before = (jnp.arange(rows)[:, None] < jnp.arange(rows)[None, :]).astype(jnp.bfloat16)
+    running = jnp.einsum("bcs,st->bct", onehot.astype(jnp.bfloat16), before, preferred_element_type=jnp.float32)
+    depth = jnp.arange(most, dtype=jnp.float32)
+    hit = onehot[:, :, None, :] & (running[:, :, None, :] == depth[None, None, :, None])
+    return hit.astype(jnp.bfloat16)
+
+
+def head_body(queries, keys, values, cluster_ids, out_weight):
+    n_seq = lax.axis_size("seq")
+    n_head = lax.axis_size("head")
+    n_dev = n_seq * n_head
+    tok_dev = cluster_ids.shape[1]
+    sub_rows = tok_dev // n_head
+    group_heads = HEADS // n_head
+    most = max(2, 2 * tok_dev // (n_head * CLUSTERS))
+    head_group = lax.axis_index("head")
+    group_ids = lax.dynamic_slice_in_dim(cluster_ids[:, :, 0], head_group * group_heads, group_heads, 0)
+    ids = lax.all_to_all(group_ids, "seq", split_axis=0, concat_axis=0, tiled=True)
+    ids = ids.reshape(n_seq * n_head, sub_rows)
+
+    def route(tensor):
+        split = tensor.reshape(sub_rows, n_dev, HD).transpose(1, 0, 2)
+        moved = lax.all_to_all(split, ("head", "seq"), split_axis=0, concat_axis=0, tiled=True)
+        return moved.reshape(n_head, n_seq, sub_rows, HD).transpose(1, 0, 2, 3).reshape(n_dev, sub_rows, HD)
+
+    table = head_slots(ids, most)
+    stacked = jnp.stack([route(queries), route(keys), route(values)])
+    packed = jnp.einsum(
+        "bcrt,xbtd->xcbrd", table, stacked, preferred_element_type=jnp.float32
+    ).astype(jnp.bfloat16)
+    packed = packed.reshape(3, CLUSTERS, n_dev * most, HD)
+    markers = jnp.sum(table.astype(jnp.float32), axis=3).transpose(1, 0, 2).reshape(CLUSTERS, n_dev * most)
+    result = attend_blocks(packed, markers).reshape(CLUSTERS, n_dev, most, HD)
+    back = jnp.einsum(
+        "bcrt,cbrd->btd", table, result, preferred_element_type=jnp.float32
+    ).astype(jnp.bfloat16)
+    back = back.reshape(n_seq, tok_dev, HD)
+    gathered = lax.all_to_all(back, "seq", split_axis=0, concat_axis=0, tiled=True)
+    gathered = gathered.transpose(1, 0, 2).reshape(tok_dev, group_heads * HD)
+    partial_value = jnp.dot(
+        gathered,
+        lax.all_gather(out_weight, "seq", axis=1, tiled=True),
+        preferred_element_type=jnp.float32,
+    )
+    return lax.psum_scatter(
+        partial_value.astype(jnp.bfloat16), "head", scatter_dimension=1, tiled=True
+    )
+
+
 def solution(mesh):
     in_specs = (
         P(("seq", "head"), None),
@@ -102,4 +154,5 @@
         P("head", "seq"),
     )
     out_specs = P("seq", "head")
+    body = head_body if mesh.size == HEADS else generic_body
     return jax.shard_map(body, mesh=mesh, in_specs=in_specs, out_specs=out_specs, check_vma=False)

time: 742 us -> 464 us (0.63)
  waiting for transfers between devices: 423 us -> 265 us
  blocking collectives: 145 us -> 50.6 us
  other arithmetic: 21.6 us -> 4.73 us
  starting transfers between devices: 25.7 us -> 17.8 us
    all_to_all x5 -> x4, waiting for transfers between devices: 368 us -> 210 us  [the longest x3 207 us: route(): lax.all_to_all(split, ('head', 'seq'), split_axis=0, concat_axis=0, tiled...]
    all_to_all x1, blocking collectives: 145 us -> 50.6 us  [head_body(): lax.all_to_all(back, 'seq', split_axis=0, concat_axis=0, tiled=True)]
    squeeze x0 -> x3, local copies, waits for them, and re-layouts: none -> 20.2 us  [the longest x1 6.77 us: attend_blocks(): packed[0]]
    sub x1 -> x0, other arithmetic: 13.4 us -> none  [attend_blocks(): raised = jnp.exp(scores - row_max)]
    convert_element_type x4 -> x0, local copies, waits for them, and re-layouts: 12.7 us -> none  [the longest x1 6.18 us: body(): packed = jnp.einsum('hltcr,xlthd->xhclrd', home_table, stacked, preferred...]
    another operation x3 -> x0, local copies, waits for them, and re-layouts: 11.9 us -> none  [body(): jnp.stack([tensor.reshape(n_head, sub_rows, group_heads, HD) for tensor i...]
    reshape x4 -> x1, local copies, waits for them, and re-layouts: 12 us -> 2.85 us  [head_body(): back = back.reshape(n_seq, tok_dev, HD)]
    sub x0 -> x1, matrix products: none -> 9 us  [attend_blocks(): raised = jnp.exp(scores - row_max)]
  transfers between devices with their start and end apart: 7 -> 6, of which waited for: 5 -> 5; matrix products, arithmetic and copies ran while one was open for 16% -> 21% of each run, Pallas kernels for 0% -> 0%
where the time goes in v1:
time: 464 us; the launch traced here: 463 us
  waiting for transfers between devices  265 us (57%)
  local copies, waits for them, and re-layouts  58 us (12%)
  matrix products  53.4 us (12%)
  blocking collectives  50.6 us (11%)
  starting transfers between devices  17.8 us (4%)
  between operations  13.5 us (3%)
  other arithmetic  4.73 us (1%)
    all_to_all x3, waiting for transfers between devices, route(): lax.all_to_all(split, ('head', 'seq'), split_axis=0, concat_axis=0, tiled...  207 us
    reduce_scatter x1, waiting for transfers between devices, head_body(): lax.psum_scatter(partial_value.astype(jnp.bfloat16), 'head', scatter_dime...  54.4 us
    all_to_all x1, blocking collectives, head_body(): lax.all_to_all(back, 'seq', split_axis=0, concat_axis=0, tiled=True)  50.6 us
    dot_general x1, matrix products, head_body(): jnp.dot(gathered, lax.all_gather(out_weight, 'seq', axis=1, tiled=True),...  14.5 us
    unnamed x15, local copies, waits for them, and re-layouts  14.4 us
    dot_general x1, matrix products, head_body(): jnp.einsum('bcrt,cbrd->btd', table, result, preferred_element_type=jnp.fl...  10.4 us
    all_to_all x3, starting transfers between devices, route(): lax.all_to_all(split, ('head', 'seq'), split_axis=0, concat_axis=0, tiled...  10.3 us
    dot_general x1, matrix products, head_body(): jnp.einsum('bcrt,xbtd->xcbrd', table, stacked, preferred_element_type=jnp...  10.2 us
  transfers between devices with their start and end apart: 6, of which 5 were waited for; matrix products, arithmetic and copies ran while one was open for 21% of the time, Pallas kernels for 0%

profile of v1, /device:TPU:0, one launch (start us, length us, event | category | flops | bytes accessed | tf_op | source)
XLA Modules:
  0.0 463.1 jit_solution(346534728485633016)
XLA Ops:
  6.5 0.0 copy-start
  6.5 0.0 all-gather.2.cloned.1.call-start
  6.5 0.7 all-gather.2.cloned.1.call-update
  7.3 0.1 copy-done
  7.4 0.6 dynamic-slice_bitcast_fusion
  8.0 7.4 %all-to-all-start = ((s32[16,1,512]{2,1,0:T(1,128)}), s32[16,1,512]{2,1,0:T(1,128)S(1)}, u32[]{:S(2)}, u32[]{:S(2)}) async-start(s32[16,1,512]{2,1,0:T(1,128)} %dynamic-slice_bitcast_fusion), calls=%async_computation | async-start | bytes 65536 | tf_op jit(solution)/shard_map/all_to_all | solution.py:116
  15.4 4.1 copy.33
  19.5 2.5 all-to-all-done
  22.0 3.4 all-to-all-start.2
  25.4 4.1 copy.36
  29.5 75.2 %all-to-all-done.2 = bf16[32,256,128]{1,2,0:T(8,128)(2,1)S(1)} async-done(((bf16[32,256,128]{1,2,0:T(8,128)(2,1)}), bf16[32,256,128]{1,2,0:T(8,128)(2,1)S(1)}, u32[]{:S(2)}, u32[]{:S(2)}) %all-to-all-start.2) | async-done | bytes 2097184 | tf_op jit(solution)/shard_map/all_to_all | solution.py:121
  104.7 3.5 all-to-all-start.3
  108.2 4.2 copy.30
  112.3 96.1 %all-to-all-done.3 = bf16[32,256,128]{1,2,0:T(8,128)(2,1)} async-done(((bf16[32,256,128]{1,2,0:T(8,128)(2,1)}), bf16[32,256,128]{1,2,0:T(8,128)(2,1)}, u32[]{:S(2)}, u32[]{:S(2)}) %all-to-all-start.3) | async-done | bytes 2097184 | tf_op jit(solution)/shard_map/all_to_all | solution.py:121
  208.4 3.5 all-to-all-start.1
  211.9 0.0 reduce-scatter.2.cloned.1.call-start
  212.0 0.1 reduce
  212.1 0.6 iota_compare_fusion.1
  212.7 3.0 copy.27
  215.7 0.0 copy-start.4
  215.7 1.0 fusion.31
  216.7 0.0 copy-start.2
  216.7 1.9 copy-done.2
  218.7 0.0 copy-done.4
  218.7 4.0 convert_reduce_fusion
  222.7 0.1 copy.29
  222.8 1.5 copy.35
  224.3 0.0 copy-start.5
  224.3 3.3 copy.38
  227.6 36.1 %all-to-all-done.1 = bf16[32,256,128]{1,2,0:T(8,128)(2,1)} async-done(((bf16[32,256,128]{1,2,0:T(8,128)(2,1)}), bf16[32,256,128]{1,2,0:T(8,128)(2,1)}, u32[]{:S(2)}, u32[]{:S(2)}) %all-to-all-start.1) | async-done | bytes 2097184 | tf_op jit(solution)/shard_map/all_to_all | solution.py:121
  263.7 3.1 copy.32
  266.8 0.0 copy-done.5
  266.8 10.2 %convert_bitcast_fusion = bf16[3,128,32,4,128]{1,4,3,0,2:T(8,128)(2,1)} fusion(f32[32,128,256]{1,2,0:T(8,128)} %copy-done.2, pred[32,128,256]{1,2,0:T(8,128)(4,1)S(1)} %copy-done.4, bf16[1,32,256,128]{2,3,0,1:T(8,128)(2,1)} %bitcast.69, bf16[1,32,256,128]{2,3,0,1:T(8,128)(2,1)S(1)} %bitcast.68, bf16[1,32,256,128]{2,3,0,1:T(8,128)(2,1)} %bitcast.71), kind=kOutput, calls=%fused_computation.8 | convolution fusion | flops 3254779904 | bytes 24117248 | tf_op jit(solution)/shard_map/bcrt,xbtd->xcbrd/dot_general | solution.py:126
  277.0 8.8 %fusion.36 = (bf16[1,128,32,4,128]{1,4,3,0,2:T(8,128)(2,1)}, bf16[1,128,32,4,128]{1,4,3,0,2:T(8,128)(2,1)}, bf16[1,128,32,4,128]{1,4,3,0,2:T(8,128)(2,1)}) fusion(bf16[3,128,32,4,128]{1,4,3,0,2:T(8,128)(2,1)} %convert_bitcast_fusion), kind=kLoop, calls=%fused_computation.40 | loop fusion | bytes 25165824 | tf_op jit(solution)/shard_map/slice | solution.py:23
  285.8 6.8 %copy.40 = bf16[128,128,128]{2,1,0:T(8,128)(2,1)} copy(bf16[128,128,128]{0,2,1:T(8,128)(2,1)} %bitcast.63) | data formatting | bytes 8388608 | tf_op jit(solution)/shard_map/squeeze | solution.py:23
  292.6 6.7 %copy.41 = bf16[128,128,128]{2,1,0:T(8,128)(2,1)} copy(bf16[128,128,128]{0,2,1:T(8,128)(2,1)} %bitcast.62) | data formatting | bytes 8388608 | tf_op jit(solution)/shard_map/squeeze | solution.py:23
  299.3 6.7 %copy.43 = bf16[128,128,128]{2,1,0:T(8,128)(2,1)} copy(bf16[128,128,128]{0,2,1:T(8,128)(2,1)} %bitcast.61) | data formatting | bytes 8388608 | tf_op jit(solution)/shard_map/squeeze | solution.py:30
  306.1 9.0 %fusion.37 = (f32[128,128]{1,0:T(8,128)S(1)}, f32[128,128,128]{1,2,0:T(8,128)}) fusion(pred[128,128]{1,0:T(8,128)(4,1)S(1)} %copy.29, bf16[128,128,128]{2,1,0:T(8,128)(2,1)} %copy.40, bf16[128,128,128]{2,1,0:T(8,128)(2,1)} %copy.41), kind=kOutput, calls=%fused_computation.41 | convolution fusion | flops 545259648 | bytes 16859136 | tf_op jit(solution)/shard_map/sub | solution.py:27
  315.1 0.0 copy-start.3
  315.1 8.2 %fusion.25 = bf16[128,128,128]{2,1,0:T(8,128)(2,1)} fusion(bf16[128,128,128]{2,1,0:T(8,128)(2,1)} %copy.43, f32[128,128,128]{1,2,0:T(8,128)} %get-tuple-element.9, f32[128,128]{1,0:T(8,128)S(1)} %get-tuple-element.8), kind=kOutput, calls=%fused_computation.31 | convolution fusion | flops 543162368 | bytes 16842752 | tf_op jit(solution)/shard_map/cqk,ckd->cqd/dot_general | solution.py:29
  323.3 0.0 copy-done.3
  323.3 10.4 %bitcast_convert_fusion = bf16[32,256,128]{2,1,0:T(8,128)(2,1)} fusion(bf16[128,32,4,128]{3,2,1,0:T(4,128)(2,1)} %bitcast.74, f32[32,128,256]{1,2,0:T(8,128)S(1)} %copy-done.3, pred[32,128,256]{1,2,0:T(8,128)(4,1)S(1)} %copy-done.4), kind=kOutput, calls=%fused_computation.24 | convolution fusion | flops 1083179008 | bytes 11534336 | tf_op jit(solution)/shard_map/bcrt,cbrd->btd/dot_general | solution.py:132
  333.8 2.9 copy.45
  336.6 50.6 %all_to_all.29 = bf16[16,512,128]{1,2,0:T(8,128)(2,1)} all-to-all(bf16[16,512,128]{1,2,0:T(8,128)(2,1)S(1)} %copy.45), channel_id=1, replica_groups=mesh['seq'=16,'head'=2] {'seq'}, dimensions={0} | all-to-all | bytes 4194304 | tf_op jit(solution)/shard_map/all_to_all | solution.py:136
  387.2 0.0 all-gather.2.cloned.1.call-done
  387.2 0.0 copy-start.1
  387.2 14.5 %convolution_convert_fusion = bf16[512,4096]{1,0:T(8,128)(2,1)} fusion(bf16[512,2048]{0,1:T(8,128)(2,1)} %bitcast.70, bf16[2048,4096]{1,0:T(8,128)(2,1)} %all-gather.2.cloned.1.call-done), kind=kOutput, calls=%fused_computation.22 | convolution fusion | flops 8592031744 | bytes 23068672 | tf_op jit(solution)/shard_map/dot_general | solution.py:138
  401.7 0.0 reduce-scatter.2.cloned.1.call-update
  401.8 54.4 %reduce-scatter.2.cloned.1.call-done = bf16[512,2048]{1,0:T(8,128)(2,1)} async-done(((bf16[512,4096]{1,0:T(8,128)(2,1)}), bf16[512,2048]{1,0:T(8,128)(2,1)}) %reduce-scatter.2.cloned.1.call-update) | async-done | bytes 2097168 | tf_op jit(solution)/shard_map/reduce_scatter | solution.py:143
  456.2 0.0 copy-done.1
  (2 shorter events, 0.0 us)
Async XLA Ops:
  6.5 0.8 copy-start
  6.5 380.7 %all-gather.2.cloned.1.call-start = ((), (), s32[]{:S(2)}) async-start(), calls=%async_computation.6 | async-start | bytes 17825792 | tf_op jit(solution)/shard_map/all_gather | solution.py:140
  8.0 14.0 %all-to-all-start = ((s32[16,1,512]{2,1,0:T(1,128)}), s32[16,1,512]{2,1,0:T(1,128)S(1)}, u32[]{:S(2)}, u32[]{:S(2)}) async-start(s32[16,1,512]{2,1,0:T(1,128)} %dynamic-slice_bitcast_fusion), calls=%async_computation | async-start | bytes 65536 | tf_op jit(solution)/shard_map/all_to_all | solution.py:116
  22.0 82.7 %all-to-all-start.2 = ((bf16[32,256,128]{1,2,0:T(8,128)(2,1)}), bf16[32,256,128]{1,2,0:T(8,128)(2,1)S(1)}, u32[]{:S(2)}, u32[]{:S(2)}) async-start(bf16[32,256,128]{1,2,0:T(8,128)(2,1)} %bitcast.66), calls=%async_computation.2 | async-start | bytes 4194304 | tf_op jit(solution)/shard_map/all_to_all | solution.py:121
  104.7 103.8 %all-to-all-start.3 = ((bf16[32,256,128]{1,2,0:T(8,128)(2,1)}), bf16[32,256,128]{1,2,0:T(8,128)(2,1)}, u32[]{:S(2)}, u32[]{:S(2)}) async-start(bf16[32,256,128]{1,2,0:T(8,128)(2,1)} %bitcast.67), calls=%async_computation.3 | async-start | bytes 4194304 | tf_op jit(solution)/shard_map/all_to_all | solution.py:121
  208.4 55.2 %all-to-all-start.1 = ((bf16[32,256,128]{1,2,0:T(8,128)(2,1)}), bf16[32,256,128]{1,2,0:T(8,128)(2,1)}, u32[]{:S(2)}, u32[]{:S(2)}) async-start(bf16[32,256,128]{1,2,0:T(8,128)(2,1)} %bitcast.65), calls=%async_computation.1 | async-start | bytes 4194304 | tf_op jit(solution)/shard_map/all_to_all | solution.py:121
  211.9 244.3 %reduce-scatter.2.cloned.1.call-start = ((), (), s32[]{:S(2)}) async-start(), calls=%async_computation.7 | async-start | bytes 6291456 | tf_op jit(solution)/shard_map/reduce_scatter | solution.py:143
  215.7 2.9 copy-start.4
  216.7 1.9 copy-start.2
  224.3 42.5 %copy-start.5 = (bf16[16,2,256,128]{2,3,1,0:T(8,128)(2,1)S(1)}, bf16[16,2,256,128]{2,3,1,0:T(8,128)(2,1)}, u32[]{:S(2)}) copy-start(bf16[16,2,256,128]{2,3,1,0:T(8,128)(2,1)} %copy.35) | copy-start | bytes 6291460
  315.1 8.2 %copy-start.3 = (f32[32,128,256]{1,2,0:T(8,128)S(1)}, f32[32,128,256]{1,2,0:T(8,128)}, u32[]{:S(2)}) copy-start(f32[32,128,256]{1,2,0:T(8,128)} %copy-done.2) | copy-start | bytes 12582916
  387.2 69.0 %copy-start.1 = (s32[32,512,1]{1,2,0:T(1,128)S(1)}, s32[32,512,1]{1,2,0:T(1,128)}, u32[]{:S(2)}) copy-start(s32[32,512,1]{1,2,0:T(1,128)} %param.8) | copy-start | bytes 196612
Sparse Core Ops, SparseCore 0:
  9.5 215.5 all-gather.1
  401.9 54.2 reduce-scatter.1

commit v2 on v0

--- a/solution.py
+++ b/solution.py
@@ -1,6 +1,10 @@
+import functools
+
 import jax
 import jax.numpy as jnp
 from jax import lax
+from jax.experimental import pallas as pl
+from jax.experimental.pallas import tpu as pltpu
 from jax.sharding import PartitionSpec as P
 
 HEADS = 32
@@ -44,7 +48,7 @@
     return lax.all_to_all(result_block, "seq", split_axis=1, concat_axis=1, tiled=True)
 
 
-def body(queries, keys, values, cluster_ids, out_weight):
+def generic_body(queries, keys, values, cluster_ids, out_weight):
     n_seq = lax.axis_size("seq")
     n_head = lax.axis_size("head")
     head_group = lax.axis_index("head")
@@ -93,6 +97,269 @@
     )
 
 
+GROUP = 16
+CHUNK = 16
+
+
+def flipped(index, mask, count):
+    total, bit = 0, 1
+    while bit < count:
+        total = total + (index // bit + mask // bit) % 2 * bit
+        bit *= 2
+    return total
+
+
+def attend_kernel(
+    n_seq, n_head, most,
+    q_ref, k_ref, v_ref, code_ref, att_ref,
+    recv, rcode, packed, marks, result, back,
+    out_sem, in_sem, code_out, code_in, back_out, back_in,
+):
+    n_dev = n_seq * n_head
+    per_group = GROUP // most
+    n_group = n_dev // per_group
+    sub = q_ref.shape[0]
+    tok = n_head * sub
+    wide = per_group * sub
+    me_s, me_x = lax.axis_index("seq"), lax.axis_index("head")
+    me = me_x * n_seq + me_s
+    block = me_s * n_head + me_x
+    my_group = block // per_group
+    slots = CLUSTERS * GROUP
+
+    def place(index):
+        return {"seq": index % n_seq, "head": index // n_seq}
+
+    def group_mask(step):
+        return step % 2 * (n_group // 2) + step // 2
+
+    def landing(source, part):
+        rows = pl.ds(pl.multiple_of(source % per_group * sub, sub), sub)
+        return recv.at[source // per_group, rows, part * HD:(part + 1) * HD]
+
+    def code_landing(source):
+        lanes = pl.ds(pl.multiple_of(source % per_group * sub, sub), sub)
+        return rcode.at[source // per_group, :, lanes]
+
+    def columns(index):
+        return pl.ds(pl.multiple_of(index * HD, HD), HD)
+
+    parts = (q_ref, k_ref, v_ref)
+
+    barrier = pltpu.get_barrier_semaphore()
+
+    def greet(step, carry):
+        pl.semaphore_signal(
+            barrier, inc=1, device_id=place((me + step) % n_dev), device_id_type=pl.DeviceIdType.MESH
+        )
+        return carry
+
+    for part, ref in enumerate(parts):
+        pltpu.make_async_copy(ref.at[:, columns(me)], landing(block, part), in_sem.at[part, block]).start()
+    pltpu.make_async_copy(code_ref.at[me], code_landing(block), code_in.at[block]).start()
+    lax.fori_loop(1, n_dev, greet, 0)
+    pl.semaphore_wait(barrier, n_dev - 1)
+
+    def target(step):
+        inner = step % 4
+        mask = group_mask(step // 4) * 2 + inner % 2 + inner // 2 * n_seq
+        return flipped(me, mask, n_dev)
+
+    def code_copy(dst):
+        return pltpu.make_async_remote_copy(
+            src_ref=code_ref.at[dst], dst_ref=code_landing(block),
+            send_sem=code_out.at[dst], recv_sem=code_in.at[block],
+            device_id=place(dst), device_id_type=pl.DeviceIdType.MESH,
+        )
+
+    def row_copy(dst, part):
+        return pltpu.make_async_remote_copy(
+            src_ref=parts[part].at[:, columns(dst)], dst_ref=landing(block, part),
+            send_sem=out_sem.at[part, dst], recv_sem=in_sem.at[part, block],
+            device_id=place(dst), device_id_type=pl.DeviceIdType.MESH,
+        )
+
+    def send(step, carry):
+        dst = target(step)
+        code_copy(dst).start()
+        for part in range(3):
+            row_copy(dst, part).start()
+        return carry
+
+    lax.fori_loop(1, n_dev, send, 0)
+
+    ones = jnp.ones((wide, HD), jnp.bfloat16)
+
+    def pack_group(step, carry):
+        group = flipped(my_group, group_mask(step), n_group)
+
+        def arrive(inner, carry):
+            source = group * per_group + inner
+            pltpu.make_async_copy(code_landing(source), code_landing(source), code_in.at[source]).wait()
+            for part in range(3):
+                pltpu.make_async_copy(landing(source, part), landing(source, part), in_sem.at[part, source]).wait()
+            return carry
+
+        lax.fori_loop(0, per_group, arrive, 0)
+
+        def pack_chunk(chunk, carry):
+            rows = lax.broadcasted_iota(jnp.int32, (CHUNK * GROUP, wide), 0) + chunk * (CHUNK * GROUP)
+            hit = jnp.where(rcode[group] == rows, 1.0, 0.0).astype(jnp.bfloat16)
+            at = (
+                pl.ds(chunk * CHUNK, CHUNK),
+                pl.ds(pl.multiple_of(group * GROUP, GROUP), GROUP),
+            )
+            data = jnp.dot(hit, recv[group], preferred_element_type=jnp.float32).astype(jnp.bfloat16)
+            packed[at[0], at[1], :] = data.reshape(CHUNK, GROUP, 3 * HD)
+            mark = jnp.dot(hit, ones, preferred_element_type=jnp.float32).astype(jnp.bfloat16)
+            marks[at[0], at[1], :] = mark.reshape(CHUNK, GROUP, HD)
+            return carry
+
+        return lax.fori_loop(0, CLUSTERS // CHUNK, pack_chunk, carry)
+
+    lax.fori_loop(0, n_group, pack_group, 0)
+
+    def attend(step, carry):
+        for inner in range(4):
+            cluster = step * 4 + inner
+            scores = lax.dot_general(
+                packed[cluster, :, HD:2 * HD], packed[cluster, :, 0:HD],
+                (((1,), (1,)), ((), ())), preferred_element_type=jnp.float32,
+            ) * HD ** (-0.5)
+            scores = jnp.where(marks[cluster].astype(jnp.float32) > 0, scores, -1e30)
+            raised = jnp.exp(scores - jnp.max(scores, axis=0, keepdims=True))
+            weights = (raised / jnp.sum(raised, axis=0, keepdims=True)).astype(jnp.bfloat16)
+            result[cluster] = lax.dot_general(
+                weights, packed[cluster, :, 2 * HD:3 * HD],
+                (((0,), (0,)), ((), ())), preferred_element_type=jnp.float32,
+            ).astype(jnp.bfloat16)
+        return carry
+
+    lax.fori_loop(0, CLUSTERS // 4, attend, 0)
+
+    seqs = per_group // n_head
+
+    def back_copy(group, part):
+        dst = group * seqs + part
+        return pltpu.make_async_remote_copy(
+            src_ref=back.at[group, part * tok:(part + 1) * tok, :], dst_ref=att_ref.at[:, columns(me_s)],
+            send_sem=back_out.at[dst], recv_sem=back_in.at[me_s],
+            device_id={"seq": dst, "head": me_x}, device_id_type=pl.DeviceIdType.MESH,
+        )
+
+    def unpack(group):
+        rows = result[:, pl.ds(pl.multiple_of(group * GROUP, GROUP), GROUP), :].reshape(slots, HD)
+        for part in range(seqs):
+            lanes = slice(part * tok, (part + 1) * tok)
+            hit = rcode[group, :, lanes] == lax.broadcasted_iota(jnp.int32, (slots, tok), 0)
+            hit = jnp.where(hit, 1.0, 0.0).astype(jnp.bfloat16)
+            turned = lax.dot_general(
+                rows, hit, (((0,), (0,)), ((), ())), preferred_element_type=jnp.float32
+            )
+            back[group, lanes, :] = turned.T.astype(jnp.bfloat16)
+
+    def send_back(step, carry):
+        group = flipped(my_group, group_mask(n_group - step), n_group)
+        unpack(group)
+        for part in range(seqs):
+            back_copy(group, part).start()
+        return carry
+
+    lax.fori_loop(1, n_group, send_back, 0)
+    unpack(my_group)
+    own = me_s % seqs
+    own_rows = pl.ds(pl.multiple_of(own * tok, tok), tok)
+    local = pltpu.make_async_copy(back.at[my_group, own_rows, :], att_ref.at[:, columns(me_s)], back_in.at[me_s])
+    local.start()
+
+    def send_near(step, carry):
+        part = (own + step) % seqs
+        dst = my_group * seqs + part
+        pltpu.make_async_remote_copy(
+            src_ref=back.at[my_group, pl.ds(pl.multiple_of(part * tok, tok), tok), :],
+            dst_ref=att_ref.at[:, columns(me_s)],
+            send_sem=back_out.at[dst], recv_sem=back_in.at[me_s],
+            device_id={"seq": dst, "head": me_x}, device_id_type=pl.DeviceIdType.MESH,
+        ).start()
+        return carry
+
+    lax.fori_loop(1, seqs, send_near, 0)
+
+    def finish_sends(step, carry):
+        dst = target(step)
+        code_copy(dst).wait_send()
+        for part in range(3):
+            row_copy(dst, part).wait_send()
+        return carry
+
+    lax.fori_loop(1, n_dev, finish_sends, 0)
+    local.wait()
+
+    def finish_back(step, carry):
+        other = (me_s + step) % n_seq
+        landed = att_ref.at[:, columns(other)]
+        pltpu.make_async_copy(landed, landed, back_in.at[other]).wait()
+        left = back.at[other // seqs, pl.ds(pl.multiple_of(other % seqs * tok, tok), tok), :]
+        pltpu.make_async_copy(left, left, back_out.at[other]).wait()
+        return carry
+
+    lax.fori_loop(1, n_seq, finish_back, 0)
+
+
+def head_body(queries, keys, values, cluster_ids, out_weight):
+    n_seq = lax.axis_size("seq")
+    n_head = lax.axis_size("head")
+    n_dev = n_seq * n_head
+    tok_dev = cluster_ids.shape[1]
+    sub_rows = tok_dev // n_head
+    group_heads = HEADS // n_head
+    most = max(2, 2 * tok_dev // (n_head * CLUSTERS))
+    per_group = GROUP // most
+    n_group = n_dev // per_group
+    wide = per_group * sub_rows
+    head_group = lax.axis_index("head")
+    block = lax.axis_index("seq") * n_head + head_group
+    ids = lax.dynamic_slice_in_dim(cluster_ids[:, :, 0], head_group * sub_rows, sub_rows, 1)
+    earlier = jnp.arange(sub_rows)[:, None] < jnp.arange(sub_rows)[None, :]
+    same = (ids[:, :, None] == ids[:, None, :]) & earlier[None]
+    ranking = jnp.sum(same.astype(jnp.int32), axis=1)
+    codes = ids * GROUP + (block % per_group) * most + ranking
+    codes = codes.reshape(HEADS, 1, sub_rows)
+    anywhere = pl.BlockSpec(memory_space=pl.ANY)
+    attended = pl.pallas_call(
+        functools.partial(attend_kernel, n_seq, n_head, most),
+        out_shape=jax.ShapeDtypeStruct((tok_dev, group_heads * HD), jnp.bfloat16),
+        in_specs=[anywhere, anywhere, anywhere, pl.BlockSpec(memory_space=pltpu.VMEM)],
+        out_specs=anywhere,
+        scratch_shapes=[
+            pltpu.VMEM((n_group, wide, 3 * HD), jnp.bfloat16),
+            pltpu.VMEM((n_group, 1, wide), jnp.int32),
+            pltpu.VMEM((CLUSTERS, n_group * GROUP, 3 * HD), jnp.bfloat16),
+            pltpu.VMEM((CLUSTERS, n_group * GROUP, HD), jnp.bfloat16),
+            pltpu.VMEM((CLUSTERS, n_group * GROUP, HD), jnp.bfloat16),
+            pltpu.VMEM((n_group, wide, HD), jnp.bfloat16),
+            pltpu.SemaphoreType.DMA((3, n_dev)),
+            pltpu.SemaphoreType.DMA((3, n_dev)),
+            pltpu.SemaphoreType.DMA((n_dev,)),
+            pltpu.SemaphoreType.DMA((n_dev,)),
+            pltpu.SemaphoreType.DMA((n_seq,)),
+            pltpu.SemaphoreType.DMA((n_seq,)),
+        ],
+        compiler_params=pltpu.CompilerParams(
+            collective_id=0, has_side_effects=True, vmem_limit_bytes=56 * 2 ** 20
+        ),
+        cost_estimate=pl.CostEstimate(flops=2 * 10 ** 10, bytes_accessed=2 * 10 ** 7, transcendentals=2 ** 21),
+    )(queries, keys, values, codes)
+    partial_value = jnp.dot(
+        attended,
+        lax.all_gather(out_weight, "seq", axis=1, tiled=True),
+        preferred_element_type=jnp.float32,
+    )
+    return lax.psum_scatter(
+        partial_value.astype(jnp.bfloat16), "head", scatter_dimension=1, tiled=True
+    )
+
+
 def solution(mesh):
     in_specs = (
         P(("seq", "head"), None),
@@ -102,4 +369,5 @@
         P("head", "seq"),
     )
     out_specs = P("seq", "head")
+    body = head_body if mesh.size == HEADS and mesh.shape["head"] == 2 else generic_body
     return jax.shard_map(body, mesh=mesh, in_specs=in_specs, out_specs=out_specs, check_vma=False)

time: 742 us -> 426 us (0.57)
  waiting for transfers between devices: 423 us -> 56.8 us
  Pallas kernels: 0 us -> 337 us
  blocking collectives: 145 us -> 0 us
  local copies, waits for them, and re-layouts: 59.5 us -> 0.77 us
  matrix products: 52.1 us -> 14.4 us
  starting transfers between devices: 25.7 us -> 0.04 us
  other arithmetic: 21.6 us -> 3.14 us
    all_to_all x5 -> x0, waiting for transfers between devices: 368 us -> none  [the longest x1 324 us: body(): lax.all_to_all(packed, 'seq', split_axis=2, concat_axis=2, tiled=True)]
    pallas_call x0 -> x1, Pallas kernels: none -> 337 us  [head_body(): pl.pallas_call(functools.partial(attend_kernel, n_seq, n_head, most), out...]
    all_to_all x1 -> x0, blocking collectives: 145 us -> none  [attend_and_return(): lax.all_to_all(result_block, 'seq', split_axis=1, concat_axis=1, tiled=True)]
    dot_general x6 -> x1, matrix products: 52.1 us -> 14.4 us  [head_body(): jnp.dot(attended, lax.all_gather(out_weight, 'seq', axis=1, tiled=True),...]
    all_to_all x5 -> x0, starting transfers between devices: 25.4 us -> none  [the longest x1 6.05 us: body(): lax.all_to_all(packed, 'seq', split_axis=2, concat_axis=2, tiled=True)]
    sub x1 -> x0, other arithmetic: 13.4 us -> none  [attend_blocks(): raised = jnp.exp(scores - row_max)]
    convert_element_type x4 -> x0, local copies, waits for them, and re-layouts: 12.7 us -> none  [the longest x1 6.18 us: body(): packed = jnp.einsum('hltcr,xlthd->xhclrd', home_table, stacked, preferred...]
    unnamed x9 -> x1, local copies, waits for them, and re-layouts: 12.3 us -> 0.01 us
  transfers between devices with their start and end apart: 7 -> 2, of which waited for: 5 -> 1; matrix products, arithmetic and copies ran while one was open for 16% -> 1% of each run, Pallas kernels for 0% -> 79%
where the time goes in v2:
time: 426 us
  Pallas kernels  337 us (79%)
  waiting for transfers between devices  56.8 us (13%)
  matrix products  14.4 us (3%)
  between operations  13.4 us (3%)
    pallas_call x1, Pallas kernels, head_body(): pl.pallas_call(functools.partial(attend_kernel, n_seq, n_head, most), out...  337 us
    reduce_scatter x1, waiting for transfers between devices, head_body(): lax.psum_scatter(partial_value.astype(jnp.bfloat16), 'head', scatter_dime...  56.1 us
    dot_general x1, matrix products, head_body(): jnp.dot(attended, lax.all_gather(out_weight, 'seq', axis=1, tiled=True),...  14.4 us
  transfers between devices with their start and end apart: 2, of which 1 were waited for; matrix products, arithmetic and copies ran while one was open for 1% of the time, Pallas kernels for 79%

profile of v2, /device:TPU:0, one launch (start us, length us, event | category | flops | bytes accessed | tf_op | source)
XLA Modules:
  0.0 425.9 jit_solution(7931516178227424585)
XLA Ops:
  6.5 0.0 all-gather.2.cloned.1.call-start
  6.5 0.7 all-gather.2.cloned.1.call-update
  7.3 0.0 reduce-scatter.2.cloned.1.call-start
  7.3 0.8 constant_dynamic-slice_fusion
  8.1 1.7 convert_reduce_fusion
  9.8 1.4 bitcast_add_fusion.code_ref
  11.2 337.3 %shard_map.55 = bf16[512,2048]{1,0:T(8,128)(2,1)} custom-call(bf16[256,4096]{1,0:T(8,128)(2,1)} %q_ref.1, bf16[256,4096]{1,0:T(8,128)(2,1)} %k_ref.1, bf16[256,4096]{1,0:T(8,128)(2,1)} %v_ref.1, s32[32,1,256]{2,1,0:T(1,128)} %bitcast_add_fusion.code_ref), custom_call_target="tpu_custom_call" | custom-call | flops 20000000000 | bytes 20000000 | tf_op jit(solution)/shard_map/pallas_call | solution.py:329
  348.5 0.0 all-gather.2.cloned.1.call-done
  348.6 14.4 %convolution_convert_fusion = bf16[512,4096]{1,0:T(8,128)(2,1)} fusion(bf16[512,2048]{1,0:T(8,128)(2,1)} %shard_map.55, bf16[2048,4096]{1,0:T(8,128)(2,1)} %all-gather.2.cloned.1.call-done), kind=kOutput, calls=%fused_computation.1 | convolution fusion | flops 8592031744 | bytes 23068672 | tf_op jit(solution)/shard_map/dot_general | solution.py:353
  363.0 0.0 reduce-scatter.2.cloned.1.call-update
  363.0 56.1 %reduce-scatter.2.cloned.1.call-done = bf16[512,2048]{1,0:T(8,128)(2,1)} async-done(((bf16[512,4096]{1,0:T(8,128)(2,1)}), bf16[512,2048]{1,0:T(8,128)(2,1)}) %reduce-scatter.2.cloned.1.call-update) | async-done | bytes 2097168 | tf_op jit(solution)/shard_map/reduce_scatter | solution.py:358
  (2 shorter events, 0.0 us)
Async XLA Ops:
  6.5 342.0 %all-gather.2.cloned.1.call-start = ((), (), s32[]{:S(2)}) async-start(), calls=%async_computation.1 | async-start | bytes 17825792 | tf_op jit(solution)/shard_map/all_gather | solution.py:355
  7.3 411.8 %reduce-scatter.2.cloned.1.call-start = ((), (), s32[]{:S(2)}) async-start(), calls=%async_computation.2 | async-start | bytes 6291456 | tf_op jit(solution)/shard_map/reduce_scatter | solution.py:358
Sparse Core Ops, SparseCore 0:
  9.5 275.5 all-gather.1
  363.1 55.9 reduce-scatter.1

commit v3 on v2

--- a/solution.py
+++ b/solution.py
@@ -111,9 +111,9 @@
 
 def attend_kernel(
     n_seq, n_head, most,
-    q_ref, k_ref, v_ref, code_ref, att_ref,
+    q_ref, k_ref, v_ref, w_ref, code_ref, att_ref, whole_ref,
     recv, rcode, packed, marks, result, back,
-    out_sem, in_sem, code_out, code_in, back_out, back_in,
+    out_sem, in_sem, code_out, code_in, back_out, back_in, weight_out, weight_in,
 ):
     n_dev = n_seq * n_head
     per_group = GROUP // most
@@ -186,7 +186,40 @@
             row_copy(dst, part).start()
         return carry
 
+    width = w_ref.shape[1]
+
+    def weight_block(index):
+        return whole_ref.at[:, pl.ds(pl.multiple_of(index * width, width), width)]
+
+    def weight_copy(stage, item):
+        mask = n_seq >> (stage + 1)
+        held = flipped(me_s, item * (2 * mask), n_seq)
+        return pltpu.make_async_remote_copy(
+            src_ref=w_ref if stage == 0 else weight_block(held), dst_ref=weight_block(held),
+            send_sem=weight_out.at[2 ** stage - 1 + item], recv_sem=weight_in.at[held],
+            device_id={"seq": flipped(me_s, mask, n_seq), "head": me_x},
+            device_id_type=pl.DeviceIdType.MESH,
+        )
+
+    stages = n_seq.bit_length() - 1
+
+    def spread(stage):
+        if stage > 0:
+            weights_arrive(stage - 1)
+        for item in range(2 ** stage):
+            weight_copy(stage, item).start()
+
+    def weights_arrive(stage):
+        mask = n_seq >> (stage + 1)
+        for item in range(2 ** stage):
+            new = flipped(me_s, item * (2 * mask) + mask, n_seq)
+            pltpu.make_async_copy(weight_block(new), weight_block(new), weight_in.at[new]).wait()
+
+    own_weight = pltpu.make_async_copy(w_ref, weight_block(me_s), weight_in.at[me_s])
+    own_weight.start()
+    spread(0)
     lax.fori_loop(1, n_dev, send, 0)
+    own_weight.wait()
 
     ones = jnp.ones((wide, HD), jnp.bfloat16)
 
@@ -217,7 +250,11 @@
 
         return lax.fori_loop(0, CLUSTERS // CHUNK, pack_chunk, carry)
 
-    lax.fori_loop(0, n_group, pack_group, 0)
+    lax.fori_loop(0, 2, pack_group, 0)
+    spread(1)
+    lax.fori_loop(2, 4, pack_group, 0)
+    spread(2)
+    lax.fori_loop(4, n_group, pack_group, 0)
 
     def attend(step, carry):
         for inner in range(4):
@@ -267,6 +304,7 @@
 
     lax.fori_loop(1, n_group, send_back, 0)
     unpack(my_group)
+    spread(3)
     own = me_s % seqs
     own_rows = pl.ds(pl.multiple_of(own * tok, tok), tok)
     local = pltpu.make_async_copy(back.at[my_group, own_rows, :], att_ref.at[:, columns(me_s)], back_in.at[me_s])
@@ -304,6 +342,10 @@
         return carry
 
     lax.fori_loop(1, n_seq, finish_back, 0)
+    weights_arrive(stages - 1)
+    for stage in range(stages):
+        for item in range(2 ** stage):
+            weight_copy(stage, item).wait_send()
 
 
 def head_body(queries, keys, values, cluster_ids, out_weight):
@@ -326,11 +368,14 @@
     codes = ids * GROUP + (block % per_group) * most + ranking
     codes = codes.reshape(HEADS, 1, sub_rows)
     anywhere = pl.BlockSpec(memory_space=pl.ANY)
-    attended = pl.pallas_call(
+    attended, whole = pl.pallas_call(
         functools.partial(attend_kernel, n_seq, n_head, most),
-        out_shape=jax.ShapeDtypeStruct((tok_dev, group_heads * HD), jnp.bfloat16),
-        in_specs=[anywhere, anywhere, anywhere, pl.BlockSpec(memory_space=pltpu.VMEM)],
-        out_specs=anywhere,
+        out_shape=(
+            jax.ShapeDtypeStruct((tok_dev, group_heads * HD), jnp.bfloat16),
+            jax.ShapeDtypeStruct((out_weight.shape[0], n_seq * out_weight.shape[1]), jnp.bfloat16),
+        ),
+        in_specs=[anywhere, anywhere, anywhere, anywhere, pl.BlockSpec(memory_space=pltpu.VMEM)],
+        out_specs=(anywhere, anywhere),
         scratch_shapes=[
             pltpu.VMEM((n_group, wide, 3 * HD), jnp.bfloat16),
             pltpu.VMEM((n_group, 1, wide), jnp.int32),
@@ -344,20 +389,28 @@
             pltpu.SemaphoreType.DMA((n_dev,)),
             pltpu.SemaphoreType.DMA((n_seq,)),
             pltpu.SemaphoreType.DMA((n_seq,)),
+            pltpu.SemaphoreType.DMA((n_seq,)),
+            pltpu.SemaphoreType.DMA((n_seq,)),
         ],
         compiler_params=pltpu.CompilerParams(
             collective_id=0, has_side_effects=True, vmem_limit_bytes=56 * 2 ** 20
         ),
         cost_estimate=pl.CostEstimate(flops=2 * 10 ** 10, bytes_accessed=2 * 10 ** 7, transcendentals=2 ** 21),
-    )(queries, keys, values, codes)
-    partial_value = jnp.dot(
-        attended,
-        lax.all_gather(out_weight, "seq", axis=1, tiled=True),
-        preferred_element_type=jnp.float32,
-    )
-    return lax.psum_scatter(
-        partial_value.astype(jnp.bfloat16), "head", scatter_dimension=1, tiled=True
-    )
+    )(queries, keys, values, out_weight, codes)
+    half = whole.shape[1] // n_head
+    piece = half // 4
+
+    def share(first, size):
+        columns = lax.dynamic_slice_in_dim(whole, first, size, 1)
+        return jnp.dot(attended, columns, preferred_element_type=jnp.float32)
+
+    theirs = (1 - head_group) * half
+    received = [
+        lax.ppermute(share(theirs + part * piece, piece).astype(jnp.bfloat16), "head", [(0, 1), (1, 0)])
+        for part in range(4)
+    ]
+    received = jnp.concatenate(received, axis=1).astype(jnp.float32)
+    return (share(head_group * half, half) + received).astype(jnp.bfloat16)
 
 
 def solution(mesh):
@@ -369,5 +422,5 @@
         P("head", "seq"),
     )
     out_specs = P("seq", "head")
-    body = head_body if mesh.size == HEADS and mesh.shape["head"] == 2 else generic_body
+    body = head_body if mesh.size == HEADS and mesh.shape["seq"] == 16 else generic_body
     return jax.shard_map(body, mesh=mesh, in_specs=in_specs, out_specs=out_specs, check_vma=False)

time: 426 us -> 381 us (0.89)
  waiting for transfers between devices: 56.8 us -> 32.7 us
  Pallas kernels: 337 us -> 316 us
  between operations: 13.4 us -> 0.06 us
  matrix products: 14.4 us -> 24.5 us
    reduce_scatter x1 -> x0, waiting for transfers between devices: 56.1 us -> none  [head_body(): lax.psum_scatter(partial_value.astype(jnp.bfloat16), 'head', scatter_dime...]
    ppermute x0 -> x4, waiting for transfers between devices: none -> 32.7 us  [head_body(): lax.ppermute(share(theirs + part * piece, piece).astype(jnp.bfloat16), 'h...]
    pallas_call x1, Pallas kernels: 337 us -> 316 us  [head_body(): pl.pallas_call(functools.partial(attend_kernel, n_seq, n_head, most), out...]
    dot_general x1 -> x5, matrix products: 14.4 us -> 24.5 us  [share(): return jnp.dot(attended, columns, preferred_element_type=jnp.float32)]
  transfers between devices with their start and end apart: 2 -> 4, of which waited for: 1 -> 3; matrix products, arithmetic and copies ran while one was open for 1% -> 3% of each run, Pallas kernels for 79% -> 0%
where the time goes in v3:
time: 381 us
  Pallas kernels  316 us (83%)
  waiting for transfers between devices  32.7 us (9%)
  matrix products  24.5 us (6%)
  starting transfers between devices  4.24 us (1%)
    pallas_call x1, Pallas kernels, head_body(): pl.pallas_call(functools.partial(attend_kernel, n_seq, n_head, most), out...  316 us
    ppermute x4, waiting for transfers between devices, head_body(): lax.ppermute(share(theirs + part * piece, piece).astype(jnp.bfloat16), 'h...  32.7 us
    dot_general x5, matrix products, share(): return jnp.dot(attended, columns, preferred_element_type=jnp.float32)  24.5 us
  transfers between devices with their start and end apart: 4, of which 3 were waited for; matrix products, arithmetic and copies ran while one was open for 3% of the time, Pallas kernels for 0%

profile of v3, /device:TPU:0, one launch (start us, length us, event | category | flops | bytes accessed | tf_op | source)
XLA Modules:
  0.0 381.2 jit_solution(3116094360105922647)
XLA Ops:
  0.0 0.8 constant_dynamic-slice_fusion
  0.8 1.7 convert_reduce_fusion
  2.5 1.4 bitcast_add_fusion.code_ref
  3.9 315.7 %shard_map.55 = (bf16[512,2048]{1,0:T(8,128)(2,1)}, bf16[2048,4096]{1,0:T(8,128)(2,1)}) custom-call(bf16[256,4096]{1,0:T(8,128)(2,1)} %q_ref.1, bf16[256,4096]{1,0:T(8,128)(2,1)} %k_ref.1, bf16[256,4096]{1,0:T(8,128)(2,1)} %v_ref.1, bf16[2048,256]{1,0:T(8,128)(2,1)} %w_ref.1, s32[32,1,256]{2,1,0:T(1,128)} %bitcast_add_fusion.code_ref), custom_call_target="tpu_custom_call" | custom-call | flops 20000000000 | bytes 20000000 | tf_op jit(solution)/shard_map/pallas_call | solution.py:371
  319.7 3.5 fusion.10
  323.1 1.7 collective-permute-start
  324.8 3.5 fusion.13
  328.3 0.5 collective-permute-start.1
  328.8 3.5 fusion.16
  332.2 1.7 collective-permute-start.2
  333.9 4.3 %fusion.19 = bf16[512,512]{1,0:T(8,128)(2,1)} fusion(bf16[512,2048]{1,0:T(8,128)(2,1)} %get-tuple-element.7, bf16[2048,4096]{1,0:T(8,128)(2,1)} %get-tuple-element.8, s32[]{:T(128)S(6)} %select_n.31), kind=kOutput, calls=%fused_computation.15 | convolution fusion | flops 1074003968 | bytes 4718596 | tf_op jit(solution)/shard_map/dot_general | solution.py:405
  338.2 0.4 collective-permute-start.3
  338.6 0.0 collective-permute-done
  338.6 10.6 %collective-permute-done.1 = bf16[512,512]{1,0:T(8,128)(2,1)S(1)} collective-permute-done((bf16[512,512]{1,0:T(8,128)(2,1)S(1)}, bf16[512,512]{1,0:T(8,128)(2,1)S(1)}, u32[]{:S(2)}, u32[]{:S(2)}) %collective-permute-start.1) | collective-permute-done | bytes 524320 | tf_op jit(solution)/shard_map/ppermute | solution.py:409
  349.2 11.2 %collective-permute-done.2 = bf16[512,512]{1,0:T(8,128)(2,1)S(1)} collective-permute-done((bf16[512,512]{1,0:T(8,128)(2,1)S(1)}, bf16[512,512]{1,0:T(8,128)(2,1)S(1)}, u32[]{:S(2)}, u32[]{:S(2)}) %collective-permute-start.2) | collective-permute-done | bytes 524320 | tf_op jit(solution)/shard_map/ppermute | solution.py:409
  360.4 10.9 %collective-permute-done.3 = bf16[512,512]{1,0:T(8,128)(2,1)} collective-permute-done((bf16[512,512]{1,0:T(8,128)(2,1)}, bf16[512,512]{1,0:T(8,128)(2,1)}, u32[]{:S(2)}, u32[]{:S(2)}) %collective-permute-start.3) | collective-permute-done | bytes 524320 | tf_op jit(solution)/shard_map/ppermute | solution.py:409
  371.3 9.9 %add_convert_fusion = bf16[512,2048]{1,0:T(8,128)(2,1)} fusion(bf16[512,512]{1,0:T(8,128)(2,1)} %collective-permute-done.3, bf16[512,512]{1,0:T(8,128)(2,1)S(1)} %collective-permute-done.2, bf16[512,512]{1,0:T(8,128)(2,1)S(1)} %collective-permute-done.1, bf16[512,512]{1,0:T(8,128)(2,1)S(1)} %collective-permute-done, bf16[512,2048]{1,0:T(8,128)(2,1)} %get-tuple-element.7, ...), kind=kOutput, calls=%fused_computation.3 | convolution fusion | flops 4305453056 | bytes 14680068 | tf_op jit(solution)/shard_map/dot_general | solution.py:405
  (2 shorter events, 0.0 us)
Async XLA Ops:
  323.1 15.5 %collective-permute-start = (bf16[512,512]{1,0:T(8,128)(2,1)S(1)}, bf16[512,512]{1,0:T(8,128)(2,1)S(1)}, u32[]{:S(2)}, u32[]{:S(2)}) collective-permute-start(bf16[512,512]{1,0:T(8,128)(2,1)S(1)} %fusion.10), channel_id=1, source_target_pairs={{0,1},{1,0},{2,3},{3,2},{4,5},{5,4},{6,7},{7,6},{8,9},{9,8},{10,11... | collective-permute-start | bytes 1572872 | tf_op jit(solution)/shard_map/ppermute | solution.py:409
  328.3 20.9 %collective-permute-start.1 = (bf16[512,512]{1,0:T(8,128)(2,1)S(1)}, bf16[512,512]{1,0:T(8,128)(2,1)S(1)}, u32[]{:S(2)}, u32[]{:S(2)}) collective-permute-start(bf16[512,512]{1,0:T(8,128)(2,1)S(1)} %fusion.13), channel_id=1, source_target_pairs={{0,1},{1,0},{2,3},{3,2},{4,5},{5,4},{6,7},{7,6},{8,9},{9,8},{10,11... | collective-permute-start | bytes 1572872 | tf_op jit(solution)/shard_map/ppermute | solution.py:409
  332.2 28.2 %collective-permute-start.2 = (bf16[512,512]{1,0:T(8,128)(2,1)S(1)}, bf16[512,512]{1,0:T(8,128)(2,1)S(1)}, u32[]{:S(2)}, u32[]{:S(2)}) collective-permute-start(bf16[512,512]{1,0:T(8,128)(2,1)S(1)} %fusion.16), channel_id=1, source_target_pairs={{0,1},{1,0},{2,3},{3,2},{4,5},{5,4},{6,7},{7,6},{8,9},{9,8},{10,11... | collective-permute-start | bytes 1572872 | tf_op jit(solution)/shard_map/ppermute | solution.py:409
  338.2 33.1 %collective-permute-start.3 = (bf16[512,512]{1,0:T(8,128)(2,1)}, bf16[512,512]{1,0:T(8,128)(2,1)}, u32[]{:S(2)}, u32[]{:S(2)}) collective-permute-start(bf16[512,512]{1,0:T(8,128)(2,1)} %fusion.19), channel_id=1, source_target_pairs={{0,1},{1,0},{2,3},{3,2},{4,5},{5,4},{6,7},{7,6},{8,9},{9,8},{10,11... | collective-permute-start | bytes 1572872 | tf_op jit(solution)/shard_map/ppermute | solution.py:409

commit v4 on v3

--- a/solution.py
+++ b/solution.py
@@ -273,6 +273,7 @@
         return carry
 
     lax.fori_loop(0, CLUSTERS // 4, attend, 0)
+    spread(3)
 
     seqs = per_group // n_head
 
@@ -304,7 +305,6 @@
 
     lax.fori_loop(1, n_group, send_back, 0)
     unpack(my_group)
-    spread(3)
     own = me_s % seqs
     own_rows = pl.ds(pl.multiple_of(own * tok, tok), tok)
     local = pltpu.make_async_copy(back.at[my_group, own_rows, :], att_ref.at[:, columns(me_s)], back_in.at[me_s])
@@ -409,8 +409,9 @@
         lax.ppermute(share(theirs + part * piece, piece).astype(jnp.bfloat16), "head", [(0, 1), (1, 0)])
         for part in range(4)
     ]
+    own = lax.optimization_barrier(share(head_group * half, half))
     received = jnp.concatenate(received, axis=1).astype(jnp.float32)
-    return (share(head_group * half, half) + received).astype(jnp.bfloat16)
+    return (own + received).astype(jnp.bfloat16)
 
 
 def solution(mesh):

time: 381 us -> 392 us (1.029)
  Pallas kernels: 316 us -> 334 us
  waiting for transfers between devices: 32.7 us -> 23.1 us
    pallas_call x1, Pallas kernels: 316 us -> 334 us  [head_body(): pl.pallas_call(functools.partial(attend_kernel, n_seq, n_head, most), out...]
    ppermute x4, waiting for transfers between devices: 32.7 us -> 23.1 us  [head_body(): lax.ppermute(share(theirs + part * piece, piece).astype(jnp.bfloat16), 'h...]
  transfers between devices with their start and end apart: 4 -> 4, of which waited for: 3 -> 3; matrix products, arithmetic and copies ran while one was open for 3% -> 5% of each run, Pallas kernels for 0% -> 0%
where the time goes in v4:
time: 392 us; the launch traced here: 391 us
  Pallas kernels  334 us (85%)
  waiting for transfers between devices  23.1 us (6%)
  matrix products  23 us (6%)
  other arithmetic  5.23 us (1%)
  starting transfers between devices  4.18 us (1%)
    pallas_call x1, Pallas kernels, head_body(): pl.pallas_call(functools.partial(attend_kernel, n_seq, n_head, most), out...  334 us
    ppermute x4, waiting for transfers between devices, head_body(): lax.ppermute(share(theirs + part * piece, piece).astype(jnp.bfloat16), 'h...  23.1 us
    dot_general x5, matrix products, share(): return jnp.dot(attended, columns, preferred_element_type=jnp.float32)  23 us
  transfers between devices with their start and end apart: 4, of which 3 were waited for; matrix products, arithmetic and copies ran while one was open for 5% of the time, Pallas kernels for 0%

profile of v4, /device:TPU:0, one launch (start us, length us, event | category | flops | bytes accessed | tf_op | source)
XLA Modules:
  0.0 390.9 jit_solution(1016585139408219141)
XLA Ops:
  0.0 0.8 constant_dynamic-slice_fusion
  0.8 1.7 convert_reduce_fusion
  2.5 1.4 bitcast_add_fusion.code_ref
  3.9 334.5 %shard_map.55 = (bf16[512,2048]{1,0:T(8,128)(2,1)}, bf16[2048,4096]{1,0:T(8,128)(2,1)}) custom-call(bf16[256,4096]{1,0:T(8,128)(2,1)} %q_ref.1, bf16[256,4096]{1,0:T(8,128)(2,1)} %k_ref.1, bf16[256,4096]{1,0:T(8,128)(2,1)} %v_ref.1, bf16[2048,256]{1,0:T(8,128)(2,1)} %w_ref.1, s32[32,1,256]{2,1,0:T(1,128)} %bitcast_add_fusion.code_ref), custom_call_target="tpu_custom_call" | custom-call | flops 20000000000 | bytes 20000000 | tf_op jit(solution)/shard_map/pallas_call | solution.py:371
  338.4 3.5 fusion.10
  341.9 1.4 collective-permute-start
  343.3 3.5 fusion.13
  346.7 0.8 collective-permute-start.1
  347.5 4.3 %fusion.16 = bf16[512,512]{1,0:T(8,128)(2,1)} fusion(bf16[512,2048]{1,0:T(8,128)(2,1)} %get-tuple-element.7, bf16[2048,4096]{1,0:T(8,128)(2,1)} %get-tuple-element.8, s32[]{:T(128)S(6)} %select_n.30), kind=kOutput, calls=%fused_computation.14 | convolution fusion | flops 1074003968 | bytes 4718596 | tf_op jit(solution)/shard_map/dot_general | solution.py:405
  351.8 1.3 collective-permute-start.2
  353.1 4.3 %fusion.19 = bf16[512,512]{1,0:T(8,128)(2,1)} fusion(bf16[512,2048]{1,0:T(8,128)(2,1)} %get-tuple-element.7, bf16[2048,4096]{1,0:T(8,128)(2,1)} %get-tuple-element.8, s32[]{:T(128)S(6)} %select_n.31), kind=kOutput, calls=%fused_computation.15 | convolution fusion | flops 1074003968 | bytes 4718596 | tf_op jit(solution)/shard_map/dot_general | solution.py:405
  357.3 0.7 collective-permute-start.3
  358.1 7.6 %fusion = f32[512,2048]{1,0:T(8,128)S(1)} fusion(bf16[512,2048]{1,0:T(8,128)(2,1)} %get-tuple-element.7, bf16[2048,4096]{1,0:T(8,128)(2,1)} %get-tuple-element.8, s32[]{:T(128)S(6)} %select_n.27), kind=kOutput, calls=%fused_computation | convolution fusion | flops 4294967296 | bytes 14680068 | tf_op jit(solution)/shard_map/dot_general | solution.py:405
  365.7 0.0 collective-permute-done
  365.7 0.7 collective-permute-done.1
  366.3 11.2 %collective-permute-done.2 = bf16[512,512]{1,0:T(8,128)(2,1)S(1)} collective-permute-done((bf16[512,512]{1,0:T(8,128)(2,1)}, bf16[512,512]{1,0:T(8,128)(2,1)S(1)}, u32[]{:S(2)}, u32[]{:S(2)}) %collective-permute-start.2) | collective-permute-done | bytes 524320 | tf_op jit(solution)/shard_map/ppermute | solution.py:409
  377.6 11.2 %collective-permute-done.3 = bf16[512,512]{1,0:T(8,128)(2,1)S(1)} collective-permute-done((bf16[512,512]{1,0:T(8,128)(2,1)}, bf16[512,512]{1,0:T(8,128)(2,1)S(1)}, u32[]{:S(2)}, u32[]{:S(2)}) %collective-permute-start.3) | collective-permute-done | bytes 524320 | tf_op jit(solution)/shard_map/ppermute | solution.py:409
  388.8 2.1 add_convert_fusion
  (2 shorter events, 0.0 us)
Async XLA Ops:
  341.9 23.8 %collective-permute-start = (bf16[512,512]{1,0:T(8,128)(2,1)S(1)}, bf16[512,512]{1,0:T(8,128)(2,1)S(1)}, u32[]{:S(2)}, u32[]{:S(2)}) collective-permute-start(bf16[512,512]{1,0:T(8,128)(2,1)S(1)} %fusion.10), channel_id=1, source_target_pairs={{0,1},{1,0},{2,3},{3,2},{4,5},{5,4},{6,7},{7,6},{8,9},{9,8},{10,11... | collective-permute-start | bytes 1572872 | tf_op jit(solution)/shard_map/ppermute | solution.py:409
  346.7 19.6 %collective-permute-start.1 = (bf16[512,512]{1,0:T(8,128)(2,1)S(1)}, bf16[512,512]{1,0:T(8,128)(2,1)S(1)}, u32[]{:S(2)}, u32[]{:S(2)}) collective-permute-start(bf16[512,512]{1,0:T(8,128)(2,1)S(1)} %fusion.13), channel_id=1, source_target_pairs={{0,1},{1,0},{2,3},{3,2},{4,5},{5,4},{6,7},{7,6},{8,9},{9,8},{10,11... | collective-permute-start | bytes 1572872 | tf_op jit(solution)/shard_map/ppermute | solution.py:409
  351.8 25.8 %collective-permute-start.2 = (bf16[512,512]{1,0:T(8,128)(2,1)}, bf16[512,512]{1,0:T(8,128)(2,1)S(1)}, u32[]{:S(2)}, u32[]{:S(2)}) collective-permute-start(bf16[512,512]{1,0:T(8,128)(2,1)} %fusion.16), channel_id=1, source_target_pairs={{0,1},{1,0},{2,3},{3,2},{4,5},{5,4},{6,7},{7,6},{8,9},{9,8},{10,11... | collective-permute-start | bytes 1572872 | tf_op jit(solution)/shard_map/ppermute | solution.py:409
  357.3 31.5 %collective-permute-start.3 = (bf16[512,512]{1,0:T(8,128)(2,1)}, bf16[512,512]{1,0:T(8,128)(2,1)S(1)}, u32[]{:S(2)}, u32[]{:S(2)}) collective-permute-start(bf16[512,512]{1,0:T(8,128)(2,1)} %fusion.19), channel_id=1, source_target_pairs={{0,1},{1,0},{2,3},{3,2},{4,5},{5,4},{6,7},{7,6},{8,9},{9,8},{10,11... | collective-permute-start | bytes 1572872 | tf_op jit(solution)/shard_map/ppermute | solution.py:409
